TPU v7x, 32 devices: a whole 2x2x4 slice. The times are simulated.
32 devices in a mesh: feeder: 2 (over y), tm: 16 (over z, x, core).
Axes of the slice: x: 2, y: 2, z: 4, core: 2. Of those that a mesh axis runs over, the one named last changes fastest.
Arguments:
- observed: bfloat16 [6144, 8192], P('feeder', 'tm'), may hold values from -6 to 6
- mask_words: int32 [6144, 1024], P('feeder', 'tm'), may hold values from 0 to 255, as said below
- feeder_factor: float32 [6144, 64], P('feeder'), may hold values from -6 to 6
- time_factor: float32 [64, 8192], P(None, 'tm'), may hold values from -0.75 to 0.75
- ar_weight: float32 [10, 64], replicated, may hold values from -0.5 to 0.5
- lags: int32 [10], replicated, may hold values from 1 to 1440, as said below
- moment_first: float32 [6144, 64], P(('feeder', 'tm')), may hold values from -0.6 to 0.6
- moment_second: float32 [6144, 64], P(('feeder', 'tm')), may hold values from 0.01 to 1
Outputs:
- new_factor: float32 [6144, 64], P(('feeder', 'tm'))
- new_first: float32 [6144, 64], P(('feeder', 'tm'))
- new_second: float32 [6144, 64], P(('feeder', 'tm'))
- time_grad: float32 [64, 8192], P('feeder', 'tm')
Inputs may be any that keep to these rules, and one draw needn't show every extreme that they name: `mask_words`: bit b of word w of a feeder's row tells whether minute 8 w + b is observed (1) or not (0). Eight lags of 1 to 12, one lag between 30 and 90, and one lag of exactly 1440; lags may repeat.
All inputs are finite; a program needn't handle non-finite values.
Results may differ from a plain program's by a relative error of at most 0.00065.
Values sent between devices are 32-bit elements; how exact they have to be, the bound alone decides.
A program may use at most 64 MiB of HBM per device.

v0:
```python
import jax
import jax.numpy as jnp
from jax import lax
from jax.sharding import PartitionSpec as P

LAGMAX = 1440


DATA_WEIGHT = 1.0 / 64.0
LAM_F = 0.1
LAM_X = 0.01
LAM_AR = 8.0
BETA_ONE = 0.9
BETA_TWO = 0.999
BIAS_FIRST = 1.0 - 0.9**8
BIAS_SECOND = 1.0 - 0.999**8
LEARNING_RATE = 0.05
ADAM_EPS = 1e-08


def from_behind(value, axis, steps):
    count = lax.axis_size(axis)
    first, last = (max(0, -steps), min(count, count - steps))
    return lax.ppermute(value, axis, [(source, source + steps) for source in range(first, last)])


def unpack_mask(words):
    shifts = jnp.arange(8, dtype=jnp.int32)
    bits = words[:, :, None] >> shifts & 1
    return bits.reshape(words.shape[0], words.shape[1] * 8).astype(jnp.float32)


def lagged(source, offset, width):
    return lax.dynamic_slice_in_dim(source, offset, width, 1)


def ar_adjoint(rank_rows, weights, lags, column_start):
    ranks, width = rank_rows.shape
    hop_count = -(-LAGMAX // width)
    earlier = []
    for distance in range(hop_count, 0, -1):
        earlier.append(from_behind(rank_rows, "tm", distance))
    extended = jnp.concatenate(earlier + [rank_rows], axis=1)
    anchor = hop_count * width
    predicted = jnp.zeros_like(rank_rows)
    for lag_index in range(lags.shape[0]):
        predicted = predicted + weights[lag_index][:, None] * lagged(
            extended, anchor - lags[lag_index], width
        )
    columns = column_start + jnp.arange(width, dtype=jnp.int32)
    errors = jnp.where(columns[None, :] >= LAGMAX, rank_rows - predicted, 0.0)
    later = []
    for distance in range(1, hop_count + 1):
        later.append(from_behind(errors, "tm", -distance))
    ahead = jnp.concatenate([errors] + later, axis=1)
    carried = jnp.zeros_like(rank_rows)
    for lag_index in range(lags.shape[0]):
        carried = carried + weights[lag_index][:, None] * lagged(ahead, lags[lag_index], width)
    return errors - carried


def per_device(
    observed, mask_words, feeder_factor, time_factor, ar_weight, lags, moment_first, moment_second
):
    feeder_rows, span_dev = observed.shape
    ranks = time_factor.shape[0]
    observed_mask = unpack_mask(mask_words)
    factor_half = feeder_factor.astype(jnp.bfloat16)
    time_half = time_factor.astype(jnp.bfloat16)
    predicted = jnp.dot(factor_half, time_half, preferred_element_type=jnp.float32)
    residual = (observed_mask * (predicted - observed.astype(jnp.float32))).astype(jnp.bfloat16)
    factor_part = DATA_WEIGHT * lax.dot_general(
        residual, time_half, (((1,), (1,)), ((), ())), preferred_element_type=jnp.float32
    )
    time_part = DATA_WEIGHT * lax.dot_general(
        factor_half, residual, (((0,), (0,)), ((), ())), preferred_element_type=jnp.float32
    )
    tm_count = lax.axis_size("tm")
    tm_place = lax.axis_index("tm")
    share_rows = feeder_rows // tm_count
    grad_share = lax.psum_scatter(factor_part, "tm", scatter_dimension=0, tiled=True)
    own_factor = lax.dynamic_slice_in_dim(feeder_factor, tm_place * share_rows, share_rows, 0)
    factor_grad = grad_share + LAM_F * own_factor
    new_first = BETA_ONE * moment_first + (1.0 - BETA_ONE) * factor_grad
    new_second = BETA_TWO * moment_second + (1.0 - BETA_TWO) * factor_grad * factor_grad
    update = (
        LEARNING_RATE * (new_first / BIAS_FIRST) / (jnp.sqrt(new_second / BIAS_SECOND) + ADAM_EPS)
    )
    new_factor = own_factor - update
    feeder_count = lax.axis_size("feeder")
    feeder_place = lax.axis_index("feeder")
    band = ranks // feeder_count
    column_start = tm_place * span_dev
    time_total = lax.psum(time_part, "feeder")
    adjoint = ar_adjoint(time_factor, ar_weight, lags, column_start)
    full_grad = time_total + LAM_AR * adjoint + LAM_X * time_factor
    time_grad = lax.dynamic_slice_in_dim(full_grad, feeder_place * band, band, 0)
    return (new_factor, new_first, new_second, time_grad)


def solution(mesh):
    placed = (
        P("feeder", "tm"),
        P("feeder", "tm"),
        P("feeder", None),
        P(None, "tm"),
        P(),
        P(),
        P(("feeder", "tm"), None),
        P(("feeder", "tm"), None),
    )
    return jax.shard_map(
        per_device,
        mesh=mesh,
        in_specs=placed,
        out_specs=(
            P(("feeder", "tm"), None),
            P(("feeder", "tm"), None),
            P(("feeder", "tm"), None),
            P("feeder", "tm"),
        ),
        check_vma=False,
    )
```

profile of v0, /device:TPU:0, one launch (start us, length us, event | category | flops | bytes accessed | tf_op | source)
XLA Modules:
  0.0 110.6 jit_solution(13675736244933220997)
XLA Ops:
  8.0 0.0 copy-start
  8.0 0.0 all-reduce.2.cloned.1.call-start
  8.1 4.4 %collective-permute-start = (f32[64,512]{1,0:T(8,128)}, f32[64,512]{1,0:T(8,128)S(1)}, u32[]{:S(2)}, u32[]{:S(2)}) collective-permute-start(f32[64,512]{1,0:T(8,128)} %param.11), channel_id=1, source_target_pairs={{0,3},{1,4},{2,5},{3,6},{4,7},{5,8},{6,9},{7,10},{8,11},{9,12},{10... | collective-permute-start | bytes 393224 | tf_op jit(solution)/shard_map/ppermute | solution.py:24
  12.5 3.5 %collective-permute-start.1 = (f32[64,512]{1,0:T(8,128)}, f32[64,512]{1,0:T(8,128)S(1)}, u32[]{:S(2)}, u32[]{:S(2)}) collective-permute-start(f32[64,512]{1,0:T(8,128)} %param.11), channel_id=1, source_target_pairs={{0,2},{1,3},{2,4},{3,5},{4,6},{5,7},{6,8},{7,9},{8,10},{9,11},{10,... | collective-permute-start | bytes 393224 | tf_op jit(solution)/shard_map/ppermute | solution.py:24
  16.0 2.3 %collective-permute-start.2 = (f32[64,512]{1,0:T(8,128)}, f32[64,512]{1,0:T(8,128)S(1)}, u32[]{:S(2)}, u32[]{:S(2)}) collective-permute-start(f32[64,512]{1,0:T(8,128)} %param.11), channel_id=1, source_target_pairs={{0,1},{1,2},{2,3},{3,4},{4,5},{5,6},{6,7},{7,8},{8,9},{9,10},{10,1... | collective-permute-start | bytes 393224 | tf_op jit(solution)/shard_map/ppermute | solution.py:24
  18.3 0.0 copy-done
  18.3 3.5 %broadcast_bitcast_fusion = s32[3072,512]{0,1:T(8,128)} fusion(s32[3072,64]{0,1:T(8,128)S(1)} %copy-done), kind=kLoop, calls=%fused_computation.2 | loop fusion | bytes 7077888 | tf_op jit(solution)/shard_map/shift_right_arithmetic | solution.py:29
  21.8 0.0 copy-start.2
  21.8 0.0 copy-start.3
  21.8 6.6 %copy.14 = s32[3072,512]{1,0:T(8,128)} copy(s32[3072,512]{0,1:T(8,128)} %broadcast_bitcast_fusion) | data formatting | bytes 12582912 | tf_op jit(solution)/shard_map/shift_right_arithmetic | solution.py:29
  28.5 0.1 shift_right_arithmetic.23
  28.5 0.0 copy-done.2
  28.6 0.0 copy-done.3
  28.6 5.5 %multiply_convert_fusion = bf16[3072,512]{1,0:T(8,128)(2,1)S(1)} fusion(bf16[3072,512]{1,0:T(8,128)(2,1)} %param.8, s32[3072,512]{1,0:T(8,128)} %copy.14, s32[512]{0:T(512)S(1)} %shift_right_arithmetic.23, f32[3072,64]{0,1:T(8,128)S(1)} %copy-done.2, f32[64,512]{1,0:T(8,128)S(1)} %copy-done.3), kind=kOutput, calls=%fused_computation | convolution fusion | flops 212566016 | bytes 13502464 | tf_op jit(solution)/shard_map/dot_general | solution.py:70
  34.1 0.0 copy-start.1
  34.1 1.6 %copy-done.1 = bf16[3072,512]{1,0:T(8,128)(2,1)} copy-done((bf16[3072,512]{1,0:T(8,128)(2,1)}, bf16[3072,512]{1,0:T(8,128)(2,1)S(1)}, u32[]{:S(2)}) %copy-start.1) | copy-done | bytes 3145752
  35.7 1.3 %fusion = f32[64,512]{1,0:T(8,128)} fusion(bf16[3072,512]{1,0:T(8,128)(2,1)S(1)} %multiply_convert_fusion, f32[3072,64]{0,1:T(8,128)S(1)} %copy-done.2), kind=kOutput, calls=%fused_computation.4 | convolution fusion | flops 201555968 | bytes 4063232 | tf_op jit(solution)/shard_map/dot_general | solution.py:75
  37.1 0.0 copy-start.7
  37.1 0.0 copy-start.6
  37.1 0.0 all-reduce.2.cloned.1.call-update
  37.1 0.0 reduce-scatter.4.cloned.1.call-start
  37.1 3.0 %convolution_multiply_fusion = f32[3072,64]{0,1:T(8,128)S(1)} fusion(bf16[3072,512]{1,0:T(8,128)(2,1)} %copy-done.1, f32[64,512]{1,0:T(8,128)S(1)} %copy-done.3), kind=kOutput, calls=%fused_computation.1 | convolution fusion | flops 201555968 | bytes 4063232 | tf_op jit(solution)/shard_map/dot_general | solution.py:72
  40.1 0.0 copy-start.4
  40.1 0.0 copy-start.5
  40.1 1.6 %copy.15 = f32[3072,64]{1,0:T(8,128)} copy(f32[3072,64]{0,1:T(8,128)S(1)} %convolution_multiply_fusion) | data formatting | bytes 1572864
  41.8 0.0 reduce-scatter.4.cloned.1.call-update
  41.8 0.0 copy-done.7
  41.8 0.0 copy-done.6
  41.8 0.7 fusion.10
  55.3 0.0 collective-permute-done
  55.3 0.0 collective-permute-done.1
  55.4 0.0 collective-permute-done.2
  55.4 0.6 subtract_select_fusion
  56.0 1.3 %collective-permute-start.5 = (f32[64,512]{1,0:T(8,128)S(1)}, f32[64,512]{1,0:T(8,128)S(1)}, u32[]{:S(2)}, u32[]{:S(2)}) collective-permute-start(f32[64,512]{1,0:T(8,128)S(1)} %subtract_select_fusion), channel_id=1, source_target_pairs={{3,0},{4,1},{5,2},{6,3},{7,4},{8,5},{9,6},{10,7},{11,8},{12,9},{13... | collective-permute-start | bytes 393224 | tf_op jit(solution)/shard_map/ppermute | solution.py:24
  57.3 1.3 %collective-permute-start.4 = (f32[64,512]{1,0:T(8,128)S(1)}, f32[64,512]{1,0:T(8,128)S(1)}, u32[]{:S(2)}, u32[]{:S(2)}) collective-permute-start(f32[64,512]{1,0:T(8,128)S(1)} %subtract_select_fusion), channel_id=1, source_target_pairs={{2,0},{3,1},{4,2},{5,3},{6,4},{7,5},{8,6},{9,7},{10,8},{11,9},{12,... | collective-permute-start | bytes 393224 | tf_op jit(solution)/shard_map/ppermute | solution.py:24
  58.6 1.3 %collective-permute-start.3 = (f32[64,512]{1,0:T(8,128)S(1)}, f32[64,512]{1,0:T(8,128)S(1)}, u32[]{:S(2)}, u32[]{:S(2)}) collective-permute-start(f32[64,512]{1,0:T(8,128)S(1)} %subtract_select_fusion), channel_id=1, source_target_pairs={{1,0},{2,1},{3,2},{4,3},{5,4},{6,5},{7,6},{8,7},{9,8},{10,9},{11,1... | collective-permute-start | bytes 393224 | tf_op jit(solution)/shard_map/ppermute | solution.py:24
  72.6 0.1 dynamic-slice
  79.0 0.0 collective-permute-done.5
  79.1 0.0 collective-permute-done.4
  79.1 0.0 collective-permute-done.3
  79.1 0.5 multiply_add_fusion
  79.6 0.0 all-reduce.2.cloned.1.call-done
  79.6 1.6 %fusion.4 = f32[32,512]{1,0:T(8,128)} fusion(f32[64,512]{1,0:T(8,128)S(1)} %copy-done.3, s32[]{:T(128)S(6)} %select_n.92, f32[64,512]{1,0:T(8,128)} %all-reduce.2.cloned.1.call-done, f32[64,512]{1,0:T(8,128)S(1)} %subtract_select_fusion, f32[64,2048]{1,0:T(8,128)S(1)} %pad_maximum_fusion, s32[]{:T(128)S(6)} %select_n.91, f32[64,512]{1,0:T(8,128)S(1)} %get-tuple-element.8, ...), kind=kLoop, calls=%fused_computation.14 | loop fusion | flops 131072 | bytes 458888 | tf_op jit(solution)/shard_map/add | solution.py:96
  81.2 20.1 %reduce-scatter.4.cloned.1.call-done = f32[192,64]{1,0:T(8,128)} async-done(((f32[3072,64]{1,0:T(8,128)}), f32[192,64]{1,0:T(8,128)}) %reduce-scatter.4.cloned.1.call-update) | async-done | bytes 49168
  101.3 1.0 copy.16
  102.3 0.0 copy-done.4
  102.3 0.0 copy-done.5
  102.3 0.8 divide_subtract_fusion
  (8 shorter events, 0.1 us)
Async XLA Ops:
  8.0 10.3 %copy-start = (s32[3072,64]{0,1:T(8,128)S(1)}, s32[3072,64]{0,1:T(8,128)}, u32[]{:S(2)}) copy-start(s32[3072,64]{0,1:T(8,128)} %param.9) | copy-start | bytes 2359300
  8.0 71.6 %all-reduce.2.cloned.1.call-start = ((), (), s32[]{:S(2)}) async-start(), calls=%async_computation.1 | async-start | bytes 262144 | tf_op jit(solution)/shard_map/psum | solution.py:94
  8.1 47.2 %collective-permute-start = (f32[64,512]{1,0:T(8,128)}, f32[64,512]{1,0:T(8,128)S(1)}, u32[]{:S(2)}, u32[]{:S(2)}) collective-permute-start(f32[64,512]{1,0:T(8,128)} %param.11), channel_id=1, source_target_pairs={{0,3},{1,4},{2,5},{3,6},{4,7},{5,8},{6,9},{7,10},{8,11},{9,12},{10... | collective-permute-start | bytes 393224 | tf_op jit(solution)/shard_map/ppermute | solution.py:24
  12.5 42.8 %collective-permute-start.1 = (f32[64,512]{1,0:T(8,128)}, f32[64,512]{1,0:T(8,128)S(1)}, u32[]{:S(2)}, u32[]{:S(2)}) collective-permute-start(f32[64,512]{1,0:T(8,128)} %param.11), channel_id=1, source_target_pairs={{0,2},{1,3},{2,4},{3,5},{4,6},{5,7},{6,8},{7,9},{8,10},{9,11},{10,... | collective-permute-start | bytes 393224 | tf_op jit(solution)/shard_map/ppermute | solution.py:24
  16.0 39.4 %collective-permute-start.2 = (f32[64,512]{1,0:T(8,128)}, f32[64,512]{1,0:T(8,128)S(1)}, u32[]{:S(2)}, u32[]{:S(2)}) collective-permute-start(f32[64,512]{1,0:T(8,128)} %param.11), channel_id=1, source_target_pairs={{0,1},{1,2},{2,3},{3,4},{4,5},{5,6},{6,7},{7,8},{8,9},{9,10},{10,1... | collective-permute-start | bytes 393224 | tf_op jit(solution)/shard_map/ppermute | solution.py:24
  21.8 6.7 %copy-start.2 = (f32[3072,64]{0,1:T(8,128)S(1)}, f32[3072,64]{0,1:T(8,128)}, u32[]{:S(2)}) copy-start(f32[3072,64]{0,1:T(8,128)} %param.10) | copy-start | bytes 2359300
  21.8 6.7 %copy-start.3 = (f32[64,512]{1,0:T(8,128)S(1)}, f32[64,512]{1,0:T(8,128)}, u32[]{:S(2)}) copy-start(f32[64,512]{1,0:T(8,128)} %param.11) | copy-start | bytes 393220
  34.1 1.6 %copy-start.1 = (bf16[3072,512]{1,0:T(8,128)(2,1)}, bf16[3072,512]{1,0:T(8,128)(2,1)S(1)}, u32[]{:S(2)}) copy-start(bf16[3072,512]{1,0:T(8,128)(2,1)S(1)} %multiply_convert_fusion) | copy-start | bytes 9437188
  37.1 4.7 %copy-start.7 = (f32[10,64]{1,0:T(8,128)S(1)}, f32[10,64]{1,0:T(8,128)}, u32[]{:S(2)}) copy-start(f32[10,64]{1,0:T(8,128)} %param.12) | copy-start | bytes 7684
  37.1 4.8 %copy-start.6 = (s32[10]{0:T(128)S(1)}, s32[10]{0:T(128)}, u32[]{:S(2)}) copy-start(s32[10]{0:T(128)} %param.13) | copy-start | bytes 124
  37.1 64.3 %reduce-scatter.4.cloned.1.call-start = ((), (), s32[]{:S(2)}) async-start(), calls=%async_computation.2 | async-start | bytes 1671168
  40.1 62.2 %copy-start.4 = (f32[192,64]{0,1:T(8,128)S(1)}, f32[192,64]{0,1:T(8,128)}, u32[]{:S(2)}) copy-start(f32[192,64]{0,1:T(8,128)} %param.14) | copy-start | bytes 147460
  40.1 62.2 %copy-start.5 = (f32[192,64]{0,1:T(8,128)S(1)}, f32[192,64]{0,1:T(8,128)}, u32[]{:S(2)}) copy-start(f32[192,64]{0,1:T(8,128)} %param.15) | copy-start | bytes 147460
  56.0 23.1 %collective-permute-start.5 = (f32[64,512]{1,0:T(8,128)S(1)}, f32[64,512]{1,0:T(8,128)S(1)}, u32[]{:S(2)}, u32[]{:S(2)}) collective-permute-start(f32[64,512]{1,0:T(8,128)S(1)} %subtract_select_fusion), channel_id=1, source_target_pairs={{3,0},{4,1},{5,2},{6,3},{7,4},{8,5},{9,6},{10,7},{11,8},{12,9},{13... | collective-permute-start | bytes 393224 | tf_op jit(solution)/shard_map/ppermute | solution.py:24
  57.3 21.8 %collective-permute-start.4 = (f32[64,512]{1,0:T(8,128)S(1)}, f32[64,512]{1,0:T(8,128)S(1)}, u32[]{:S(2)}, u32[]{:S(2)}) collective-permute-start(f32[64,512]{1,0:T(8,128)S(1)} %subtract_select_fusion), channel_id=1, source_target_pairs={{2,0},{3,1},{4,2},{5,3},{6,4},{7,5},{8,6},{9,7},{10,8},{11,9},{12,... | collective-permute-start | bytes 393224 | tf_op jit(solution)/shard_map/ppermute | solution.py:24
  58.6 20.5 %collective-permute-start.3 = (f32[64,512]{1,0:T(8,128)S(1)}, f32[64,512]{1,0:T(8,128)S(1)}, u32[]{:S(2)}, u32[]{:S(2)}) collective-permute-start(f32[64,512]{1,0:T(8,128)S(1)} %subtract_select_fusion), channel_id=1, source_target_pairs={{1,0},{2,1},{3,2},{4,3},{5,4},{6,5},{7,6},{8,7},{9,8},{10,9},{11,1... | collective-permute-start | bytes 393224 | tf_op jit(solution)/shard_map/ppermute | solution.py:24
Sparse Core Ops, SparseCore 0:
  37.2 21.5 all-reduce.1
Sparse Core Ops, SparseCore 1:
  41.9 59.4 reduce-scatter.3
where the time goes:
time: 111 us
  between operations  47.6 us (43%)
  waiting for transfers between devices  20.2 us (18%)
  local copies, waits for them, and re-layouts  15.3 us (14%)
  starting transfers between devices  14.2 us (13%)
  matrix products  9.8 us (9%)
  other arithmetic  3.44 us (3%)
    unnamed x3, waiting for transfers between devices  20.2 us
    ppermute x6, starting transfers between devices, from_behind(): lax.ppermute(value, axis, [(source, source + steps) for source in range(f...  14.1 us
    shift_right_arithmetic x4, local copies, waits for them, and re-layouts, unpack_mask(): bits = words[:, :, None] >> shifts & 1  10.2 us
    dot_general x1, matrix products, per_device(): jnp.dot(factor_half, time_half, preferred_element_type=jnp.float32)  5.53 us
    unnamed x21, local copies, waits for them, and re-layouts  4.32 us
    dot_general x1, matrix products, per_device(): lax.dot_general(residual, time_half, (((1,), (1,)), ((), ())), preferred_...  2.95 us
  transfers between devices with their start and end apart: 8, of which 1 were waited for; matrix products, arithmetic and copies ran while one was open for 23% of the time, Pallas kernels for 0%

commit v1 on v0

v1 whole, which is shorter than its diff:
```python
import functools

import jax
import jax.numpy as jnp
from jax import lax
from jax.experimental import pallas as pl
from jax.experimental.pallas import tpu as pltpu
from jax.sharding import PartitionSpec as P

LAGMAX = 1440
LANES = 128
MESH = pl.DeviceIdType.MESH

DATA_WEIGHT = 1.0 / 64.0
LAM_F = 0.1
LAM_X = 0.01
LAM_AR = 8.0
BETA_ONE = 0.9
BETA_TWO = 0.999
BIAS_FIRST = 1.0 - 0.9**8
BIAS_SECOND = 1.0 - 0.999**8
LEARNING_RATE = 0.05
ADAM_EPS = 1e-08


def xor(a, b, count):
    total = 0
    bit = 1
    while bit < count:
        total = total + bit * ((a // bit + b // bit) % 2)
        bit *= 2
    return total


def halo_pieces(span):
    blocks = span // LANES
    far = -(-LAGMAX // LANES)
    wanted = (
        list(range(-far, blocks + 2 - far))
        + list(range(-1, blocks + 1))
        + list(range(far - 2, far + blocks))
    )
    pieces = []
    for slot, block in enumerate(wanted):
        distance, place = divmod(block, blocks)
        if distance == 0:
            continue
        last = pieces[-1] if pieces else None
        if last and last[0] == distance and last[1] + last[3] == place and last[2] + last[3] == slot:
            last[3] += 1
        else:
            pieces.append([distance, place, slot, 1])
    return pieces, len(wanted)


def kernel(
    feeders, tms, chunk, share,
    obs_hbm, words_hbm, factor_hbm, time_ref, weight_ref, lags_ref, first_ref, second_ref,
    new_factor_ref, new_first_ref, new_second_ref, time_grad_ref,
    obs, words, factor, rhs_wide, rhs_back, window, weights,
    parts, pair, sums, landed, time_part, time_landed,
    in_sem, pair_send, pair_recv, sum_send, sum_recv, time_send, time_recv, halo_send, halo_recv,
):
    ranks, span = time_ref.shape
    rows = obs_hbm.shape[0]
    steps = rows // chunk
    members = chunk // share
    pairs = members // 2
    half = share // 2
    band = ranks // feeders
    f = lax.axis_index("feeder")
    tm = lax.axis_index("tm")
    core = tm % 2
    my_chunk = tm // members
    my_pair = (tm // 2) % pairs
    partner = tm + 1 - 2 * core
    band_rows = pl.ds(pl.multiple_of(f * band, 8), band)
    pieces, slots = halo_pieces(span)
    blocks = span // LANES

    def loads(s):
        start = pl.multiple_of(xor(my_chunk, steps - 1 - s, steps) * chunk, LANES)
        where = pl.ds(start, chunk)
        return (
            pltpu.make_async_copy(obs_hbm.at[where, :], obs.at[s], in_sem.at[0, s]),
            pltpu.make_async_copy(words_hbm.at[:, where], words.at[s], in_sem.at[1, s]),
            pltpu.make_async_copy(factor_hbm.at[:, where], factor.at[s], in_sem.at[2, s]),
        )

    for s in range(steps):
        for copy in loads(s):
            copy.start()

    window[...] = jnp.zeros_like(window)
    barrier = pltpu.get_barrier_semaphore()

    @pl.loop(1, tms)
    def _(k):
        pl.semaphore_signal(barrier, inc=1, device_id=(f, (tm + k) % tms), device_id_type=MESH)

    for k in range(1, feeders):
        pl.semaphore_signal(barrier, inc=1, device_id=((f + k) % feeders, tm), device_id_type=MESH)

    time_all = time_ref[...]
    time_zero = jnp.zeros_like(time_all)
    wide = span // 8
    column = lax.broadcasted_iota(jnp.int32, (wide, span), 1)
    word = lax.broadcasted_iota(jnp.int32, (wide, span), 0)
    level = jnp.left_shift(jnp.int32(1), 7 - jnp.bitwise_and(column, 7)).astype(jnp.float32) * (1.0 / 128.0)
    spread = jnp.where(jnp.right_shift(column, 3) == word, level, 0.0)
    rhs_wide[0:ranks, 0:span] = time_all.astype(jnp.bfloat16)
    rhs_wide[0:ranks, span : 2 * span] = jnp.zeros((ranks, span), jnp.bfloat16)
    rhs_wide[ranks : ranks + wide, 0:span] = jnp.zeros((wide, span), jnp.bfloat16)
    rhs_wide[ranks : ranks + wide, span : 2 * span] = spread.astype(jnp.bfloat16)
    rhs_back[0:span, :] = jnp.concatenate([time_all, time_zero], axis=0).T.astype(jnp.bfloat16)
    rhs_back[span : 2 * span, :] = jnp.concatenate([time_zero, time_all], axis=0).T.astype(jnp.bfloat16)
    time_part[...] = jnp.zeros_like(time_part)

    def pair_copy(s, j):
        return pltpu.make_async_remote_copy(
            src_ref=parts.at[s, 2 * j + 1 - core], dst_ref=pair.at[s, j],
            send_sem=pair_send.at[s, j], recv_sem=pair_recv.at[s, j],
            device_id=(f, partner), device_id_type=MESH,
        )

    def sum_copy(s, j, slot):
        target = (xor(my_chunk, steps - 1 - s, steps) * pairs + j) * 2 + core
        return pltpu.make_async_remote_copy(
            src_ref=sums.at[s, j], dst_ref=landed.at[s, slot],
            send_sem=sum_send.at[s, j], recv_sem=sum_recv.at[s, slot],
            device_id=(f, target), device_id_type=MESH,
        )

    def halo_copy(index):
        distance, place, slot, count = pieces[index]
        return pltpu.make_async_remote_copy(
            src_ref=time_ref.at[band_rows, pl.ds(place * LANES, count * LANES)],
            dst_ref=window.at[:, pl.ds(slot * LANES, count * LANES)],
            send_sem=halo_send.at[index], recv_sem=halo_recv.at[index],
            device_id=(f, (tm - distance + tms) % tms), device_id_type=MESH,
        )

    def halo_goes(index):
        to = tm - pieces[index][0]
        return jnp.logical_and(to >= 0, to < tms)

    def halo_comes(index):
        source = tm + pieces[index][0]
        return jnp.logical_and(source >= 0, source < tms)

    def time_copy(k):
        peer = (f + k) % feeders
        return pltpu.make_async_remote_copy(
            src_ref=time_part.at[pl.ds(pl.multiple_of(peer * band, 8), band), :],
            dst_ref=time_landed.at[k - 1],
            send_sem=time_send.at[k - 1], recv_sem=time_recv.at[k - 1],
            device_id=(peer, tm), device_id_type=MESH,
        )

    def forward(s):
        for j in range(pairs):
            pair_copy(s, j).wait_recv()
            sums[s, j] = parts[s, 2 * j + core] + pair[s, j]
            sum_copy(s, j, my_pair).start()

    def step(s, carry):
        for copy in loads(s):
            copy.wait()
        factor_t = factor[s]
        both = jnp.concatenate([factor_t, words[s].astype(jnp.float32)], axis=0).T.astype(jnp.bfloat16)
        product = jnp.dot(both, rhs_wide[...], preferred_element_type=jnp.float32)
        bits = jnp.bitwise_and(product[:, span:].astype(jnp.int32), 1)
        exact = jnp.where(bits == 1, product[:, :span] - obs[s].astype(jnp.float32), 0.0)
        residual = exact.astype(jnp.bfloat16)
        cut = residual if half % 16 == 0 else exact
        left = jnp.concatenate([cut[d * share : d * share + half] for d in range(members)], axis=0)
        right = jnp.concatenate([cut[d * share + half : (d + 1) * share] for d in range(members)], axis=0)
        stacked = jnp.concatenate([left, right], axis=1).astype(jnp.bfloat16)
        grads = jnp.dot(stacked, rhs_back[...], preferred_element_type=jnp.float32)
        for d in range(members):
            parts[s, d] = grads[d * half : (d + 1) * half]
        time_part[...] += jnp.dot(factor_t.astype(jnp.bfloat16), residual, preferred_element_type=jnp.float32)

        @pl.when(s == 0)
        def _():
            pl.semaphore_wait(barrier, tms - 1 + feeders - 1)
            for index in range(len(pieces)):
                @pl.when(halo_goes(index))
                def _(index=index):
                    halo_copy(index).start()

        for j in range(pairs):
            pair_copy(s, j).start()

        @pl.when(s >= 1)
        def _():
            forward(s - 1)

        return carry

    lax.fori_loop(0, steps, step, 0)
    last = steps - 1
    for k in range(1, feeders):
        time_copy(k).start()

    time_own = time_ref[band_rows, :]
    for index in range(len(pieces)):
        @pl.when(halo_comes(index))
        def _(index=index):
            halo_copy(index).wait_recv()

    third = slots // 3 * LANES
    own_at = third + LANES
    window[:, own_at : own_at + span] = time_own
    weights[...] = jnp.zeros_like(weights)
    lag_count = weight_ref.shape[0]
    weights[0:ranks, 0:lag_count] = weight_ref[...].T
    weight = weights[band_rows, :]
    far = -(-LAGMAX // LANES)
    ahead = far * LANES - LAGMAX
    errors_width = span + LANES
    past = window[:, 0:third]
    mid = window[:, third : 2 * third]
    future = window[:, 2 * third : 3 * third]
    short, shifts = [], []
    long = jnp.zeros((band, 1), jnp.float32)
    for index in range(lag_count):
        lag = lags_ref[index]
        here = weight[:, index : index + 1]
        is_long = lag >= LANES
        short.append(jnp.where(is_long, 0.0, here))
        long = long + jnp.where(is_long, here, 0.0)
        shifts.append(jnp.where(is_long, 0, lag))
    near = long * pltpu.roll(past, third - ahead, 1)[:, 0:errors_width]
    later = long * pltpu.roll(mid, third - ahead, 1)[:, 0:errors_width]
    for index in range(lag_count):
        near = near + short[index] * pltpu.roll(mid, shifts[index], 1)[:, LANES:]
        later = later + short[index] * pltpu.roll(future, shifts[index], 1)[:, LANES:]
    columns = lax.broadcasted_iota(jnp.int32, (band, errors_width), 1) + tm * span
    errors = jnp.where(
        jnp.logical_and(columns >= LAGMAX, columns < tms * span), mid[:, LANES:] - near, 0.0
    )
    later_columns = columns + (far - 1) * LANES
    later_errors = jnp.where(
        jnp.logical_and(later_columns >= LAGMAX, later_columns < tms * span), future[:, LANES:] - later, 0.0
    )
    carried = long * pltpu.roll(later_errors, errors_width - (LANES - ahead), 1)[:, 0:span]
    for index in range(lag_count):
        carried = carried + short[index] * pltpu.roll(errors, errors_width - shifts[index], 1)[:, 0:span]
    adjoint = errors[:, 0:span] - carried
    regular = LAM_AR * adjoint + LAM_X * time_own

    for j in range(pairs):
        pair_copy(last, j).wait_recv()
        sums[last, j] = parts[last, 2 * j + core] + pair[last, j]
        if pairs > 1:
            @pl.when(j != my_pair)
            def _(j=j):
                sum_copy(last, j, my_pair).start()

    total = sums[last, my_pair]
    for s in range(steps):
        for j in range(pairs):
            if s < last:
                sum_copy(s, j, j).wait_recv()
                total = total + landed[s, j]
            elif pairs > 1:
                @pl.when(j != my_pair)
                def _(j=j):
                    sum_copy(last, j, j).wait_recv()

                total = total + jnp.where(j == my_pair, 0.0, landed[last, j])
    turned = total.T
    gradient = jnp.concatenate([turned[0:ranks], turned[ranks : 2 * ranks]], axis=1)
    own_chunk = factor[last]
    own = own_chunk[:, 0:share]
    for d in range(1, members):
        own = jnp.where(tm % members == d, own_chunk[:, d * share : (d + 1) * share], own)
    gradient = DATA_WEIGHT * gradient + LAM_F * own
    new_first = BETA_ONE * first_ref[...] + (1.0 - BETA_ONE) * gradient
    new_second = BETA_TWO * second_ref[...] + (1.0 - BETA_TWO) * gradient * gradient
    update = (
        LEARNING_RATE * (new_first / BIAS_FIRST) / (jnp.sqrt(new_second / BIAS_SECOND) + ADAM_EPS)
    )
    new_first_ref[...] = new_first
    new_second_ref[...] = new_second
    new_factor_ref[...] = own - update

    data = time_part[band_rows, :]
    for k in range(1, feeders):
        time_copy(k).wait_recv()
        data = data + time_landed[k - 1]
    time_grad_ref[...] = DATA_WEIGHT * data + regular

    for index in range(len(pieces)):
        @pl.when(halo_goes(index))
        def _(index=index):
            halo_copy(index).wait_send()

    for k in range(1, feeders):
        time_copy(k).wait_send()
    for s in range(steps):
        for j in range(pairs):
            pair_copy(s, j).wait_send()
            if s < last:
                sum_copy(s, j, my_pair).wait_send()
            elif pairs > 1:
                @pl.when(j != my_pair)
                def _(s=s, j=j):
                    sum_copy(s, j, my_pair).wait_send()


def per_device(
    observed, mask_words, feeder_factor, time_factor, ar_weight, lags, moment_first, moment_second
):
    rows, span = observed.shape
    ranks = time_factor.shape[0]
    tms = lax.axis_size("tm")
    feeders = lax.axis_size("feeder")
    share = rows // tms
    members = 2
    while members * share % LANES:
        members *= 2
    chunk = members * share
    steps = rows // chunk
    pairs = members // 2
    half = share // 2
    band = ranks // feeders
    pieces, slots = halo_pieces(span)
    f32 = jnp.float32
    block = (half, 2 * ranks)
    dma = pltpu.SemaphoreType.DMA
    vmem = pl.BlockSpec(memory_space=pltpu.VMEM)
    hbm = pl.BlockSpec(memory_space=pl.ANY)
    flops = 2 * rows * span * ranks * 4
    new_factor, new_first, new_second, time_grad = pl.pallas_call(
        functools.partial(kernel, feeders, tms, chunk, share),
        out_shape=[jax.ShapeDtypeStruct((ranks, share), f32)] * 3
        + [jax.ShapeDtypeStruct((band, span), f32)],
        in_specs=[hbm, hbm, hbm, vmem, vmem, pl.BlockSpec(memory_space=pltpu.SMEM), vmem, vmem],
        out_specs=[vmem] * 4,
        scratch_shapes=[
            pltpu.VMEM((steps, chunk, span), jnp.bfloat16),
            pltpu.VMEM((steps, span // 8, chunk), jnp.int32),
            pltpu.VMEM((steps, ranks, chunk), f32),
            pltpu.VMEM((ranks + span // 8, 2 * span), jnp.bfloat16),
            pltpu.VMEM((2 * span, 2 * ranks), jnp.bfloat16),
            pltpu.VMEM((band, slots * LANES), f32),
            pltpu.VMEM((ranks, LANES), f32),
            pltpu.VMEM((steps, members) + block, f32),
            pltpu.VMEM((steps, pairs) + block, f32),
            pltpu.VMEM((steps, pairs) + block, f32),
            pltpu.VMEM((steps, pairs) + block, f32),
            pltpu.VMEM((ranks, span), f32),
            pltpu.VMEM((feeders - 1, band, span), f32),
            dma((3, steps)),
            dma((steps, pairs)),
            dma((steps, pairs)),
            dma((steps, pairs)),
            dma((steps, pairs)),
            dma((feeders - 1,)),
            dma((feeders - 1,)),
            dma((len(pieces),)),
            dma((len(pieces),)),
        ],
        compiler_params=pltpu.CompilerParams(
            collective_id=0, has_side_effects=True, vmem_limit_bytes=40 * 1024 * 1024
        ),
        cost_estimate=pl.CostEstimate(flops=flops, bytes_accessed=rows * span * 3, transcendentals=0),
    )(
        observed, mask_words.T, feeder_factor.T, time_factor, ar_weight, lags,
        moment_first.T, moment_second.T,
    )
    return (new_factor.T, new_first.T, new_second.T, time_grad)


def solution(mesh):
    placed = (
        P("feeder", "tm"),
        P("feeder", "tm"),
        P("feeder", None),
        P(None, "tm"),
        P(),
        P(),
        P(("feeder", "tm"), None),
        P(("feeder", "tm"), None),
    )
    return jax.shard_map(
        per_device,
        mesh=mesh,
        in_specs=placed,
        out_specs=(
            P(("feeder", "tm"), None),
            P(("feeder", "tm"), None),
            P(("feeder", "tm"), None),
            P("feeder", "tm"),
        ),
        check_vma=False,
    )
```

time: 111 us -> 33.6 us (0.30)
  between operations: 47.6 us -> 0.66 us
  Pallas kernels: 0 us -> 21.9 us
  waiting for transfers between devices: 20.2 us -> 0 us
  starting transfers between devices: 14.2 us -> 0 us
  matrix products: 9.8 us -> 0 us
  local copies, waits for them, and re-layouts: 15.3 us -> 10.6 us
  other arithmetic: 3.44 us -> 0 us
    pallas_call x0 -> x1, Pallas kernels: none -> 21.9 us  [per_device(): pl.pallas_call(functools.partial(kernel, feeders, tms, chunk, share), out...]
    unnamed x3 -> x0, waiting for transfers between devices: 20.2 us -> none
    ppermute x6 -> x0, starting transfers between devices: 14.1 us -> none  [from_behind(): lax.ppermute(value, axis, [(source, source + steps) for source in range(f...]
    shift_right_arithmetic x4 -> x0, local copies, waits for them, and re-layouts: 10.2 us -> none  [unpack_mask(): bits = words[:, :, None] >> shifts & 1]
    dot_general x3 -> x0, matrix products: 9.8 us -> none  [the longest x1 5.53 us: per_device(): jnp.dot(factor_half, time_half, preferred_element_type=jnp.float32)]
    unnamed x21 -> x20, local copies, waits for them, and re-layouts: 4.32 us -> 10.6 us
    add x2 -> x0, other arithmetic: 2.05 us -> none  [the longest x1 1.58 us: per_device(): full_grad = time_total + LAM_AR * adjoint + LAM_X * time_factor]
  transfers between devices with their start and end apart: 8 -> 0, of which waited for: 1 -> 0; matrix products, arithmetic and copies ran while one was open for 23% -> 0% of each run, Pallas kernels for 0% -> 0%
where the time goes in v1:
time: 33.6 us; the launch traced here: 33.2 us
  Pallas kernels  21.9 us (65%)
  local copies, waits for them, and re-layouts  10.6 us (32%)
  between operations  0.66 us (2%)
    pallas_call x1, Pallas kernels, per_device(): pl.pallas_call(functools.partial(kernel, feeders, tms, chunk, share), out...  21.9 us
    unnamed x20, local copies, waits for them, and re-layouts  10.6 us

profile of v1, /device:TPU:0, one launch (start us, length us, event | category | flops | bytes accessed | tf_op | source)
XLA Modules:
  0.0 33.2 jit_solution(5994869946059181985)
XLA Ops:
  0.6 0.0 copy-start
  0.6 1.9 %copy-done = bf16[3072,512]{1,0:T(8,128)(2,1)S(1)} copy-done((bf16[3072,512]{1,0:T(8,128)(2,1)S(1)}, bf16[3072,512]{1,0:T(8,128)(2,1)}, u32[]{:S(2)}) %copy-start) | copy-done | bytes 3145752
  2.5 0.0 copy-start.1
  2.5 1.1 %copy-done.1 = s32[3072,64]{0,1:T(8,128)S(1)} copy-done((s32[3072,64]{0,1:T(8,128)S(1)}, s32[3072,64]{0,1:T(8,128)}, u32[]{:S(2)}) %copy-start.1) | copy-done | bytes 786456
  3.7 0.0 copy-start.2
  3.7 1.1 %copy-done.2 = f32[3072,64]{0,1:T(8,128)S(1)} copy-done((f32[3072,64]{0,1:T(8,128)S(1)}, f32[3072,64]{0,1:T(8,128)}, u32[]{:S(2)}) %copy-start.2) | copy-done | bytes 786456
  4.8 0.0 copy-start.3
  4.8 0.9 %copy-done.3 = f32[64,512]{1,0:T(8,128)S(1)} copy-done((f32[64,512]{1,0:T(8,128)S(1)}, f32[64,512]{1,0:T(8,128)}, u32[]{:S(2)}) %copy-start.3) | copy-done | bytes 131096
  5.7 0.0 copy-start.4
  5.7 0.8 %copy-done.4 = f32[192,64]{0,1:T(8,128)S(1)} copy-done((f32[192,64]{0,1:T(8,128)S(1)}, f32[192,64]{0,1:T(8,128)}, u32[]{:S(2)}) %copy-start.4) | copy-done | bytes 49176
  6.5 0.0 copy-start.5
  6.5 0.8 %copy-done.5 = f32[192,64]{0,1:T(8,128)S(1)} copy-done((f32[192,64]{0,1:T(8,128)S(1)}, f32[192,64]{0,1:T(8,128)}, u32[]{:S(2)}) %copy-start.5) | copy-done | bytes 49176
  7.4 0.0 copy-start.6
  7.4 0.7 %copy-done.6 = f32[10,64]{1,0:T(8,128)S(1)} copy-done((f32[10,64]{1,0:T(8,128)S(1)}, f32[10,64]{1,0:T(8,128)}, u32[]{:S(2)}) %copy-start.6) | copy-done | bytes 2584
  8.1 0.0 copy-start.7
  8.1 0.7 %copy-done.7 = s32[10]{0:T(128)S(1)} copy-done((s32[10]{0:T(128)S(1)}, s32[10]{0:T(128)}, u32[]{:S(2)}) %copy-start.7) | copy-done | bytes 64
  8.7 21.9 %shard_map.111 = (f32[64,192]{1,0:T(8,128)S(1)}, f32[64,192]{1,0:T(8,128)S(1)}, f32[64,192]{1,0:T(8,128)S(1)}, f32[32,512]{1,0:T(8,128)S(1)}) custom-call(bf16[3072,512]{1,0:T(8,128)(2,1)S(1)} %copy-done, s32[64,3072]{1,0:T(8,128)S(1)} %bitcast.7, f32[64,3072]{1,0:T(8,128)S(1)} %bitcast.8, f32[64,512]{1,0:T(8,128)S(1)} %copy-done.3, f32[10,64]{1,0:T(8,128)S(1)} %copy-done.6, ...), custom_call_target="tpu_custom_call" | custom-call | flops 805306368 | bytes 4718592 | tf_op jit(solution)/shard_map/pallas_call | solution.py:336
  30.7 0.6 %copy.16 = f32[192,64]{0,1:T(8,128)} copy(f32[192,64]{0,1:T(8,128)S(1)} %bitcast.13) | data formatting | bytes 98304
  31.3 0.6 %copy.17 = f32[192,64]{0,1:T(8,128)} copy(f32[192,64]{0,1:T(8,128)S(1)} %bitcast.12) | data formatting | bytes 98304
  31.9 0.6 %copy.18 = f32[192,64]{0,1:T(8,128)} copy(f32[192,64]{0,1:T(8,128)S(1)} %bitcast.11) | data formatting | bytes 98304
  32.6 0.6 %copy.19 = f32[32,512]{1,0:T(8,128)} copy(f32[32,512]{1,0:T(8,128)S(1)} %get-tuple-element.19) | data formatting | bytes 131072
Async XLA Ops:
  0.6 1.9 %copy-start = (bf16[3072,512]{1,0:T(8,128)(2,1)S(1)}, bf16[3072,512]{1,0:T(8,128)(2,1)}, u32[]{:S(2)}) copy-start(bf16[3072,512]{1,0:T(8,128)(2,1)} %obs_hbm.1) | copy-start | bytes 9437188
  2.5 1.1 %copy-start.1 = (s32[3072,64]{0,1:T(8,128)S(1)}, s32[3072,64]{0,1:T(8,128)}, u32[]{:S(2)}) copy-start(s32[3072,64]{0,1:T(8,128)} %param.9) | copy-start | bytes 2359300
  3.7 1.1 %copy-start.2 = (f32[3072,64]{0,1:T(8,128)S(1)}, f32[3072,64]{0,1:T(8,128)}, u32[]{:S(2)}) copy-start(f32[3072,64]{0,1:T(8,128)} %param.10) | copy-start | bytes 2359300
  4.8 0.9 %copy-start.3 = (f32[64,512]{1,0:T(8,128)S(1)}, f32[64,512]{1,0:T(8,128)}, u32[]{:S(2)}) copy-start(f32[64,512]{1,0:T(8,128)} %time_ref.1) | copy-start | bytes 393220
  5.7 0.8 %copy-start.4 = (f32[192,64]{0,1:T(8,128)S(1)}, f32[192,64]{0,1:T(8,128)}, u32[]{:S(2)}) copy-start(f32[192,64]{0,1:T(8,128)} %param.14) | copy-start | bytes 147460
  6.5 0.8 %copy-start.5 = (f32[192,64]{0,1:T(8,128)S(1)}, f32[192,64]{0,1:T(8,128)}, u32[]{:S(2)}) copy-start(f32[192,64]{0,1:T(8,128)} %param.15) | copy-start | bytes 147460
  7.4 0.7 %copy-start.6 = (f32[10,64]{1,0:T(8,128)S(1)}, f32[10,64]{1,0:T(8,128)}, u32[]{:S(2)}) copy-start(f32[10,64]{1,0:T(8,128)} %weight_ref.1) | copy-start | bytes 7684
  8.1 0.7 %copy-start.7 = (s32[10]{0:T(128)S(1)}, s32[10]{0:T(128)}, u32[]{:S(2)}) copy-start(s32[10]{0:T(128)} %lags_ref.1) | copy-start | bytes 124

commit v2 on v1

--- a/solution.py
+++ b/solution.py
@@ -55,11 +55,11 @@
 
 def kernel(
     feeders, tms, chunk, share,
-    obs_hbm, words_hbm, factor_hbm, time_ref, weight_ref, lags_ref, first_ref, second_ref,
+    obs_hbm, words_hbm, factor_hbm, time_hbm, weight_hbm, lags_ref, first_hbm, second_hbm,
     new_factor_ref, new_first_ref, new_second_ref, time_grad_ref,
-    obs, words, factor, rhs_wide, rhs_back, window, weights,
+    obs, words, factor, time_ref, weight_ref, first_ref, second_ref, rhs_wide, rhs_back, window, weights,
     parts, pair, sums, landed, time_part, time_landed,
-    in_sem, pair_send, pair_recv, sum_send, sum_recv, time_send, time_recv, halo_send, halo_recv,
+    in_sem, small_sem, pair_send, pair_recv, sum_send, sum_recv, time_send, time_recv, halo_send, halo_recv,
 ):
     ranks, span = time_ref.shape
     rows = obs_hbm.shape[0]
@@ -87,9 +87,18 @@
             pltpu.make_async_copy(factor_hbm.at[:, where], factor.at[s], in_sem.at[2, s]),
         )
 
+    time_load, weight_load, first_load, second_load = [
+        pltpu.make_async_copy(source, target, small_sem.at[index])
+        for index, (source, target) in enumerate(
+            [(time_hbm, time_ref), (weight_hbm, weight_ref), (first_hbm, first_ref), (second_hbm, second_ref)]
+        )
+    ]
+    time_load.start()
     for s in range(steps):
         for copy in loads(s):
             copy.start()
+    for copy in (weight_load, first_load, second_load):
+        copy.start()
 
     window[...] = jnp.zeros_like(window)
     barrier = pltpu.get_barrier_semaphore()
@@ -101,6 +110,7 @@
     for k in range(1, feeders):
         pl.semaphore_signal(barrier, inc=1, device_id=((f + k) % feeders, tm), device_id_type=MESH)
 
+    time_load.wait()
     time_all = time_ref[...]
     time_zero = jnp.zeros_like(time_all)
     wide = span // 8
@@ -212,6 +222,7 @@
     third = slots // 3 * LANES
     own_at = third + LANES
     window[:, own_at : own_at + span] = time_own
+    weight_load.wait()
     weights[...] = jnp.zeros_like(weights)
     lag_count = weight_ref.shape[0]
     weights[0:ranks, 0:lag_count] = weight_ref[...].T
@@ -277,6 +288,8 @@
     for d in range(1, members):
         own = jnp.where(tm % members == d, own_chunk[:, d * share : (d + 1) * share], own)
     gradient = DATA_WEIGHT * gradient + LAM_F * own
+    first_load.wait()
+    second_load.wait()
     new_first = BETA_ONE * first_ref[...] + (1.0 - BETA_ONE) * gradient
     new_second = BETA_TWO * second_ref[...] + (1.0 - BETA_TWO) * gradient * gradient
     update = (
@@ -308,6 +321,17 @@
                 @pl.when(j != my_pair)
                 def _(s=s, j=j):
                     sum_copy(s, j, my_pair).wait_send()
+
+
+def hand_over(a, b, c, d, a_out, b_out, c_out, d_out, sem):
+    copies = [
+        pltpu.make_async_copy(source, target, sem.at[index])
+        for index, (source, target) in enumerate([(a, a_out), (b, b_out), (c, c_out), (d, d_out)])
+    ]
+    for copy in copies:
+        copy.start()
+    for copy in copies:
+        copy.wait()
 
 
 def per_device(
@@ -333,16 +357,20 @@
     vmem = pl.BlockSpec(memory_space=pltpu.VMEM)
     hbm = pl.BlockSpec(memory_space=pl.ANY)
     flops = 2 * rows * span * ranks * 4
-    new_factor, new_first, new_second, time_grad = pl.pallas_call(
+    results = pl.pallas_call(
         functools.partial(kernel, feeders, tms, chunk, share),
         out_shape=[jax.ShapeDtypeStruct((ranks, share), f32)] * 3
         + [jax.ShapeDtypeStruct((band, span), f32)],
-        in_specs=[hbm, hbm, hbm, vmem, vmem, pl.BlockSpec(memory_space=pltpu.SMEM), vmem, vmem],
+        in_specs=[hbm, hbm, hbm, hbm, hbm, pl.BlockSpec(memory_space=pltpu.SMEM), hbm, hbm],
         out_specs=[vmem] * 4,
         scratch_shapes=[
             pltpu.VMEM((steps, chunk, span), jnp.bfloat16),
             pltpu.VMEM((steps, span // 8, chunk), jnp.int32),
             pltpu.VMEM((steps, ranks, chunk), f32),
+            pltpu.VMEM((ranks, span), f32),
+            pltpu.VMEM(ar_weight.shape, f32),
+            pltpu.VMEM((ranks, share), f32),
+            pltpu.VMEM((ranks, share), f32),
             pltpu.VMEM((ranks + span // 8, 2 * span), jnp.bfloat16),
             pltpu.VMEM((2 * span, 2 * ranks), jnp.bfloat16),
             pltpu.VMEM((band, slots * LANES), f32),
@@ -354,6 +382,7 @@
             pltpu.VMEM((ranks, span), f32),
             pltpu.VMEM((feeders - 1, band, span), f32),
             dma((3, steps)),
+            dma((4,)),
             dma((steps, pairs)),
             dma((steps, pairs)),
             dma((steps, pairs)),
@@ -364,13 +393,20 @@
             dma((len(pieces),)),
         ],
         compiler_params=pltpu.CompilerParams(
-            collective_id=0, has_side_effects=True, vmem_limit_bytes=40 * 1024 * 1024
+            collective_id=0, has_side_effects=True, vmem_limit_bytes=63 * 1024 * 1024
         ),
         cost_estimate=pl.CostEstimate(flops=flops, bytes_accessed=rows * span * 3, transcendentals=0),
     )(
         observed, mask_words.T, feeder_factor.T, time_factor, ar_weight, lags,
         moment_first.T, moment_second.T,
     )
+    new_factor, new_first, new_second, time_grad = pl.pallas_call(
+        hand_over,
+        out_shape=[jax.ShapeDtypeStruct(result.shape, f32) for result in results],
+        in_specs=[hbm] * 4,
+        out_specs=[hbm] * 4,
+        scratch_shapes=[dma((4,))],
+    )(*results)
     return (new_factor.T, new_first.T, new_second.T, time_grad)
 
 

time: 33.6 us -> 31 us (0.923)
  local copies, waits for them, and re-layouts: 10.6 us -> 0 us
  Pallas kernels: 21.9 us -> 30.2 us
    unnamed x20 -> x0, local copies, waits for them, and re-layouts: 10.6 us -> none
    pallas_call x0 -> x1, Pallas kernels: none -> 9.08 us  [per_device(): pl.pallas_call(hand_over, out_shape=[jax.ShapeDtypeStruct(result.shape, f...]
    pallas_call x1, Pallas kernels: 21.9 us -> 21.1 us  [per_device(): pl.pallas_call(functools.partial(kernel, feeders, tms, chunk, share), out...]
where the time goes in v2:
time: 31 us; the launch traced here: 30.8 us
  Pallas kernels  30.2 us (97%)
  between operations  0.64 us (2%)
    pallas_call x1, Pallas kernels, per_device(): pl.pallas_call(functools.partial(kernel, feeders, tms, chunk, share), out...  21.1 us
    pallas_call x1, Pallas kernels, per_device(): pl.pallas_call(hand_over, out_shape=[jax.ShapeDtypeStruct(result.shape, f...  9.08 us

profile of v2, /device:TPU:0, one launch (start us, length us, event | category | flops | bytes accessed | tf_op | source)
XLA Modules:
  0.0 30.8 jit_solution(5214724085560744758)
XLA Ops:
  0.6 21.1 %shard_map.111 = (f32[64,192]{1,0:T(8,128)}, f32[64,192]{1,0:T(8,128)}, f32[64,192]{1,0:T(8,128)}, f32[32,512]{1,0:T(8,128)}) custom-call(bf16[3072,512]{1,0:T(8,128)(2,1)} %obs_hbm.1, s32[64,3072]{1,0:T(8,128)} %bitcast.7, f32[64,3072]{1,0:T(8,128)} %bitcast.8, f32[64,512]{1,0:T(8,128)} %time_hbm.1, f32[10,64]{1,0:T(8,128)} %weight_hbm.1, s32[10]{0:T(128)} %lags_ref.1, ...), custom_call_target="tpu_custom_call" | custom-call | flops 805306368 | bytes 4718592 | tf_op jit(solution)/shard_map/pallas_call | solution.py:360
  21.7 9.1 %shard_map.112 = (f32[64,192]{1,0:T(8,128)}, f32[64,192]{1,0:T(8,128)}, f32[64,192]{1,0:T(8,128)}, f32[32,512]{1,0:T(8,128)}) custom-call(f32[64,192]{1,0:T(8,128)} %get-tuple-element.12.a, f32[64,192]{1,0:T(8,128)} %get-tuple-element.13.b, f32[64,192]{1,0:T(8,128)} %get-tuple-element.14.c, f32[32,512]{1,0:T(8,128)} %get-tuple-element.15.d), custom_call_target="tpu_custom_call" | custom-call | tf_op jit(solution)/shard_map/pallas_call | solution.py:403

commit v3 on v2

--- a/solution.py
+++ b/solution.py
@@ -323,14 +323,16 @@
                     sum_copy(s, j, my_pair).wait_send()
 
 
-def hand_over(a, b, c, d, a_out, b_out, c_out, d_out, sem):
-    copies = [
-        pltpu.make_async_copy(source, target, sem.at[index])
-        for index, (source, target) in enumerate([(a, a_out), (b, b_out), (c, c_out), (d, d_out)])
-    ]
-    for copy in copies:
+def hand_over(a, b, c, d, a_out, b_out, c_out, d_out, a_held, b_held, c_held, d_held, sem):
+    triples = [(a, a_held, a_out), (b, b_held, b_out), (c, c_held, c_out), (d, d_held, d_out)]
+    come = [pltpu.make_async_copy(t[0], t[1], sem.at[0, i]) for i, t in enumerate(triples)]
+    go = [pltpu.make_async_copy(t[1], t[2], sem.at[1, i]) for i, t in enumerate(triples)]
+    for copy in come:
         copy.start()
-    for copy in copies:
+    for arrival, copy in zip(come, go):
+        arrival.wait()
+        copy.start()
+    for copy in go:
         copy.wait()
 
 
@@ -405,7 +407,7 @@
         out_shape=[jax.ShapeDtypeStruct(result.shape, f32) for result in results],
         in_specs=[hbm] * 4,
         out_specs=[hbm] * 4,
-        scratch_shapes=[dma((4,))],
+        scratch_shapes=[pltpu.VMEM(result.shape, f32) for result in results] + [dma((2, 4))],
     )(*results)
     return (new_factor.T, new_first.T, new_second.T, time_grad)
 

time: 31 us -> 23.6 us (0.76)
  Pallas kernels: 30.2 us -> 22.7 us
    pallas_call x1, Pallas kernels: 9.08 us -> 1.63 us  [per_device(): pl.pallas_call(hand_over, out_shape=[jax.ShapeDtypeStruct(result.shape, f...]
where the time goes in v3:
time: 23.6 us; the launch traced here: 23.4 us
  Pallas kernels  22.7 us (96%)
  between operations  0.64 us (3%)
    pallas_call x1, Pallas kernels, per_device(): pl.pallas_call(functools.partial(kernel, feeders, tms, chunk, share), out...  21.1 us
    pallas_call x1, Pallas kernels, per_device(): pl.pallas_call(hand_over, out_shape=[jax.ShapeDtypeStruct(result.shape, f...  1.63 us

profile of v3, /device:TPU:0, one launch (start us, length us, event | category | flops | bytes accessed | tf_op | source)
XLA Modules:
  0.0 23.4 jit_solution(1866392327666613696)
XLA Ops:
  0.6 21.1 %shard_map.111 = (f32[64,192]{1,0:T(8,128)}, f32[64,192]{1,0:T(8,128)}, f32[64,192]{1,0:T(8,128)}, f32[32,512]{1,0:T(8,128)}) custom-call(bf16[3072,512]{1,0:T(8,128)(2,1)} %obs_hbm.1, s32[64,3072]{1,0:T(8,128)} %bitcast.7, f32[64,3072]{1,0:T(8,128)} %bitcast.8, f32[64,512]{1,0:T(8,128)} %time_hbm.1, f32[10,64]{1,0:T(8,128)} %weight_hbm.1, s32[10]{0:T(128)} %lags_ref.1, ...), custom_call_target="tpu_custom_call" | custom-call | flops 805306368 | bytes 4718592 | tf_op jit(solution)/shard_map/pallas_call | solution.py:362
  21.7 1.6 %shard_map.112 = (f32[64,192]{1,0:T(8,128)}, f32[64,192]{1,0:T(8,128)}, f32[64,192]{1,0:T(8,128)}, f32[32,512]{1,0:T(8,128)}) custom-call(f32[64,192]{1,0:T(8,128)} %get-tuple-element.12.a, f32[64,192]{1,0:T(8,128)} %get-tuple-element.13.b, f32[64,192]{1,0:T(8,128)} %get-tuple-element.14.c, f32[32,512]{1,0:T(8,128)} %get-tuple-element.15.d), custom_call_target="tpu_custom_call" | custom-call | tf_op jit(solution)/shard_map/pallas_call | solution.py:405
